TPU v7x, 32 devices: a whole 2x2x4 slice. The times are simulated.
32 devices in a mesh: section: 2 (over x), dp: 16 (over z, y, core).
Axes of the slice: x: 2, y: 2, z: 4, core: 2. Of those that a mesh axis runs over, the one named last changes fastest.
Arguments:
- block_input: bfloat16 [2, 1024, 1024], P(None, 'dp'), may hold values from -6 to 6
- crop_ids: int32 [2, 1024], P(None, 'dp'), may hold values from -1 to 1, as said below
- out_grad: bfloat16 [2, 1024, 1024], P(None, 'dp'), may hold values from -6 to 6
- norm1_gain: bfloat16 [2, 1024], P('section', 'dp'), may hold values from 0.099609375 to 1.8984375
- norm1_shift: bfloat16 [2, 1024], P('section', 'dp'), may hold values from -3 to 3
- w_qkv: bfloat16 [2, 1024, 3072], P('section', 'dp'), may hold values from -0.1875 to 0.1875
- w_out: bfloat16 [2, 1024, 1024], P('section', 'dp'), may hold values from -0.75 to 0.75
- b_out: bfloat16 [2, 1024], P('section', 'dp'), may hold values from -3 to 3
- norm2_gain: bfloat16 [2, 1024], P('section', 'dp'), may hold values from 0.099609375 to 1.8984375
- norm2_shift: bfloat16 [2, 1024], P('section', 'dp'), may hold values from -3 to 3
- w_up: bfloat16 [2, 1024, 4096], P('section', 'dp'), may hold values from -0.1875 to 0.1875
- b_up: bfloat16 [2, 4096], P('section', 'dp'), may hold values from -3 to 3
- w_down: bfloat16 [2, 4096, 1024], P('section', 'dp'), may hold values from -0.09375 to 0.09375
- b_down: bfloat16 [2, 1024], P('section', 'dp'), may hold values from -3 to 3
Outputs:
- layer_outputs: bfloat16 [2, 2, 1024, 1024], P('section', None, 'dp')
- input_grads: bfloat16 [2, 2, 1024, 1024], P('section', None, 'dp')
- grad_norm1_gain: float32 [2, 1024], P('section', 'dp')
- grad_norm1_shift: float32 [2, 1024], P('section', 'dp')
- grad_w_qkv: float32 [2, 1024, 3072], P('section', 'dp')
- grad_w_out: float32 [2, 1024, 1024], P('section', 'dp')
- grad_b_out: float32 [2, 1024], P('section', 'dp')
- grad_norm2_gain: float32 [2, 1024], P('section', 'dp')
- grad_norm2_shift: float32 [2, 1024], P('section', 'dp')
- grad_w_up: float32 [2, 1024, 4096], P('section', 'dp')
- grad_b_up: float32 [2, 4096], P('section', 'dp')
- grad_w_down: float32 [2, 4096, 1024], P('section', 'dp')
- grad_b_down: float32 [2, 1024], P('section', 'dp')
Inputs may be any that keep to these rules, and one draw needn't show every extreme that they name: `crop_ids`: within each block of 64 rows of one micro-batch and one device, crops are numbered from 0 in row order: first one or more global crops of 50 rows (never more than fit in 64 rows), then local crops of 10 rows that fill the remaining room but for at most two crops' worth, then padding rows marked -1; blocks are independent.
All inputs are finite; a program needn't handle non-finite values.
Results may differ from a plain program's by a relative error of at most 0.015.
Values may be sent and summed in bfloat16 or wider, within the bound.
A program may use at most 256 MiB of HBM per device.

v0:
```python
import functools

import jax
import jax.numpy as jnp
from jax import lax
from jax.experimental import pallas as pl
from jax.experimental.pallas import tpu as pltpu
from jax.sharding import PartitionSpec as P

HEAD = 64


def passed_along(x, axis, by):
    devices = lax.axis_size(axis)
    pairs = [(i, i + by) for i in range(devices) if 0 <= i + by < devices]
    return lax.ppermute(x, axis, pairs)


def norm_rows(values, gain, shift):
    centred = values - jnp.mean(values, axis=-1, keepdims=True)
    spread = jnp.mean(centred * centred, axis=-1, keepdims=True)
    return centred * lax.rsqrt(spread + 1e-06) * gain + shift


def gelu_exact(values):
    return jax.nn.gelu(values, approximate=False)


def inner_rows(left, right):
    return lax.dot_general(
        left, right, (((0,), (0,)), ((), ())), preferred_element_type=jnp.float32
    )


def times_transpose(left, right):
    return lax.dot_general(
        left, right, (((1,), (1,)), ((), ())), preferred_element_type=jnp.float32
    )


def split_heads(qkv_rows):
    model_width = qkv_rows.shape[1] // 3
    head_count = model_width // HEAD
    queries = qkv_rows[:, :model_width].reshape(-1, head_count, HEAD)
    key_rows = qkv_rows[:, model_width : 2 * model_width].reshape(-1, head_count, HEAD)
    value_rows = qkv_rows[:, 2 * model_width :].reshape(-1, head_count, HEAD)
    return (queries, key_rows, value_rows)


def head_scores(qkv_rows, crop_rows):
    queries, key_rows, value_rows = split_heads(qkv_rows)
    scores = jnp.einsum("qhd,khd->hqk", queries, key_rows, preferred_element_type=jnp.float32)
    scores = scores * HEAD ** (-0.5)
    same_crop = crop_rows[:, None] == crop_rows[None, :]
    return jnp.where(same_crop[None], scores, -1e30)


def forward_layer(layer_in, crop_rows, weights):
    gain_one, shift_one, w_qkv, w_out, b_out, gain_two, shift_two, w_up, b_up, w_down, b_down = (
        weights
    )
    row_count = layer_in.shape[0]
    normed = norm_rows(
        layer_in, gain_one.astype(jnp.float32), shift_one.astype(jnp.float32)
    ).astype(jnp.bfloat16)
    qkv_rows = jnp.dot(normed, w_qkv, preferred_element_type=jnp.float32).astype(jnp.bfloat16)
    scores = head_scores(qkv_rows, crop_rows)
    row_peak = jnp.max(scores, axis=-1, keepdims=True)
    log_total = row_peak + jnp.log(jnp.sum(jnp.exp(scores - row_peak), axis=-1, keepdims=True))
    softmax_low = jnp.exp(scores - log_total).astype(jnp.bfloat16)
    queries, key_rows, value_rows = split_heads(qkv_rows)
    mixed_heads = jnp.einsum(
        "hqk,khd->qhd", softmax_low, value_rows, preferred_element_type=jnp.float32
    )
    mixed_heads = mixed_heads.reshape(row_count, -1).astype(jnp.bfloat16)
    hidden = (
        layer_in
        + jnp.dot(mixed_heads, w_out, preferred_element_type=jnp.float32)
        + b_out.astype(jnp.float32)
    )
    squeezed = norm_rows(
        hidden, gain_two.astype(jnp.float32), shift_two.astype(jnp.float32)
    ).astype(jnp.bfloat16)
    up_rows = jnp.dot(squeezed, w_up, preferred_element_type=jnp.float32) + b_up.astype(jnp.float32)
    active = gelu_exact(up_rows).astype(jnp.bfloat16)
    result = (
        hidden
        + jnp.dot(active, w_down, preferred_element_type=jnp.float32)
        + b_down.astype(jnp.float32)
    )
    return (
        layer_in,
        normed,
        qkv_rows,
        log_total,
        mixed_heads,
        hidden,
        squeezed,
        up_rows,
        active,
        result,
    )


def backward_feed(grad_result, saved, weights):
    gain_one, shift_one, w_qkv, w_out, b_out, gain_two, shift_two, w_up, b_up, w_down, b_down = (
        weights
    )
    (
        layer_in,
        normed,
        qkv_rows,
        log_total,
        mixed_heads,
        hidden,
        squeezed,
        up_rows,
        active,
        result,
    ) = saved
    grad_branch = grad_result.astype(jnp.bfloat16)
    grad_w_down = inner_rows(active, grad_branch)
    grad_b_down = jnp.sum(grad_branch.astype(jnp.float32), axis=0)
    grad_active = times_transpose(grad_branch, w_down)
    gelu_value, gelu_pull = jax.vjp(gelu_exact, up_rows)
    grad_up = gelu_pull(grad_active)[0].astype(jnp.bfloat16)
    grad_w_up = inner_rows(squeezed, grad_up)
    grad_b_up = jnp.sum(grad_up.astype(jnp.float32), axis=0)
    grad_squeezed = times_transpose(grad_up, w_up)
    norm_value, norm_pull = jax.vjp(
        norm_rows, hidden, gain_two.astype(jnp.float32), shift_two.astype(jnp.float32)
    )
    grad_hid, grad_gain_two, grad_shift_two = norm_pull(grad_squeezed)
    grad_hidden = grad_result + grad_hid
    return (
        grad_hidden,
        (grad_gain_two, grad_shift_two, grad_w_up, grad_b_up, grad_w_down, grad_b_down),
    )


def backward_attend(grad_hidden, saved, crop_rows, weights):
    gain_one, shift_one, w_qkv, w_out, b_out, gain_two, shift_two, w_up, b_up, w_down, b_down = (
        weights
    )
    (
        layer_in,
        normed,
        qkv_rows,
        log_total,
        mixed_heads,
        hidden,
        squeezed,
        up_rows,
        active,
        result,
    ) = saved
    row_count = layer_in.shape[0]
    grad_attn = grad_hidden.astype(jnp.bfloat16)
    grad_w_out = inner_rows(mixed_heads, grad_attn)
    grad_b_out = jnp.sum(grad_attn.astype(jnp.float32), axis=0)
    grad_mixed = times_transpose(grad_attn, w_out).astype(jnp.bfloat16)
    queries, key_rows, value_rows = split_heads(qkv_rows)
    grad_mixed = grad_mixed.reshape(queries.shape)
    softmax_out = jnp.exp(head_scores(qkv_rows, crop_rows) - log_total)
    grad_soft = jnp.einsum(
        "qhd,khd->hqk", grad_mixed, value_rows, preferred_element_type=jnp.float32
    )
    grad_values = jnp.einsum(
        "hqk,qhd->khd",
        softmax_out.astype(jnp.bfloat16),
        grad_mixed,
        preferred_element_type=jnp.float32,
    )
    row_centre = jnp.sum(grad_soft * softmax_out, axis=-1, keepdims=True)
    grad_scores = (softmax_out * (grad_soft - row_centre)).astype(jnp.bfloat16)
    grad_queries = jnp.einsum(
        "hqk,khd->qhd", grad_scores, key_rows, preferred_element_type=jnp.float32
    ) * HEAD ** (-0.5)
    grad_keys = jnp.einsum(
        "hqk,qhd->khd", grad_scores, queries, preferred_element_type=jnp.float32
    ) * HEAD ** (-0.5)
    grad_qkv = jnp.concatenate(
        [
            grad_queries.reshape(row_count, -1),
            grad_keys.reshape(row_count, -1),
            grad_values.reshape(row_count, -1),
        ],
        axis=1,
    ).astype(jnp.bfloat16)
    grad_w_qkv = inner_rows(normed, grad_qkv)
    grad_normed = times_transpose(grad_qkv, w_qkv)
    first_value, first_pull = jax.vjp(
        norm_rows, layer_in, gain_one.astype(jnp.float32), shift_one.astype(jnp.float32)
    )
    grad_in, grad_gain_one, grad_shift_one = first_pull(grad_normed)
    return (
        grad_hidden + grad_in,
        (grad_gain_one, grad_shift_one, grad_w_qkv, grad_w_out, grad_b_out),
    )


def local(
    block_input,
    crop_ids,
    out_grad,
    norm1_gain,
    norm1_shift,
    w_qkv,
    w_out,
    b_out,
    norm2_gain,
    norm2_shift,
    w_up,
    b_up,
    w_down,
    b_down,
):
    is_first = lax.axis_index("section") == 0
    shards = (
        norm1_gain,
        norm1_shift,
        w_qkv,
        w_out,
        b_out,
        norm2_gain,
        norm2_shift,
        w_up,
        b_up,
        w_down,
        b_down,
    )
    gathered = (
        lax.all_gather(shards[0], "dp", axis=1, tiled=True),
        lax.all_gather(shards[1], "dp", axis=1, tiled=True),
        lax.all_gather(shards[2], "dp", axis=1, tiled=True),
        lax.all_gather(shards[3], "dp", axis=1, tiled=True),
        lax.all_gather(shards[4], "dp", axis=1, tiled=True),
        lax.all_gather(shards[5], "dp", axis=1, tiled=True),
        lax.all_gather(shards[6], "dp", axis=1, tiled=True),
        lax.all_gather(shards[7], "dp", axis=1, tiled=True),
        lax.all_gather(shards[8], "dp", axis=1, tiled=True),
        lax.all_gather(shards[9], "dp", axis=1, tiled=True),
        lax.all_gather(shards[10], "dp", axis=1, tiled=True),
    )
    weights = tuple((item[0] for item in gathered))
    micro_count = block_input.shape[0]

    def pick(upper, lower):
        return jax.tree.map(
            lambda later, earlier: jnp.where(is_first, earlier, later), upper, lower
        )

    incoming = jnp.zeros(block_input.shape[1:], jnp.bfloat16)
    records = []
    kept_saved = []
    forward_rows = []
    for step_index in range(micro_count + 1):
        own_rows = block_input[min(step_index, micro_count - 1)]
        source = jnp.where(is_first, own_rows, incoming)
        crop_rows = jnp.where(
            is_first, crop_ids[min(step_index, micro_count - 1)], crop_ids[max(step_index - 1, 0)]
        )
        saved = forward_layer(source.astype(jnp.float32), crop_rows, weights)
        sent_rows = saved[-1].astype(jnp.bfloat16)
        forward_rows.append(sent_rows)
        records.append((source, crop_rows))
        kept_saved.append(saved)
        if step_index < micro_count:
            incoming = passed_along(sent_rows, "section", 1)
    layer_outputs = jnp.where(
        is_first, jnp.stack(forward_rows[:micro_count]), jnp.stack(forward_rows[1:])
    )
    totals = jax.tree.map(lambda item: jnp.zeros(item.shape, jnp.float32), weights)
    back_in = jnp.zeros(block_input.shape[1:], jnp.bfloat16)
    backward_rows = []
    for step_index in range(micro_count + 1):
        late_tick = min(step_index + 1, micro_count)
        early_tick = max(step_index - 1, 0)
        source, crop_rows = pick(records[late_tick], records[early_tick])
        saved = pick(kept_saved[late_tick], kept_saved[early_tick])
        if step_index < micro_count:
            last_grad = out_grad[step_index]
        else:
            last_grad = jnp.zeros_like(out_grad[0])
        cotangent = jnp.where(is_first, back_in, last_grad)
        grad_hidden, feed_grads = backward_feed(cotangent.astype(jnp.float32), saved, weights)
        feed_totals = tuple((left + right for left, right in zip(totals[5:], feed_grads)))
        grad_in, attend_grads = backward_attend(grad_hidden, saved, crop_rows, weights)
        attend_totals = tuple((left + right for left, right in zip(totals[:5], attend_grads)))
        totals = attend_totals + feed_totals
        sent_grad = grad_in.astype(jnp.bfloat16)
        backward_rows.append(sent_grad)
        if step_index < micro_count:
            back_in = passed_along(sent_grad, "section", -1)
    input_grads = jnp.where(
        is_first, jnp.stack(backward_rows[1:]), jnp.stack(backward_rows[:micro_count])
    )
    summed = lax.psum_scatter(totals, "dp", scatter_dimension=0, tiled=True)
    outputs = tuple((item[None] for item in summed))
    return (layer_outputs[None], input_grads[None]) + outputs


MESH = pl.DeviceIdType.MESH
F = jnp.float32
B = jnp.bfloat16
VECTORS = ("g1", "s1", "bo", "g2", "s2", "bd", "bu")
PARTS = (
    (4, 0, 16, False, False),
    (0, 0, 32, False, False), (0, 32, 32, False, False),
    (1, 0, 64, True, False),
    (2, 0, 32, False, True), (2, 32, 32, True, False),
    (3, 0, 128, False, False), (3, 128, 128, True, False),
)
AHEAD = 4
SUMS = (
    (3, 0, 128, True, False), (3, 128, 128, False, True),
    (2, 0, 32, True, False), (2, 32, 32, False, False),
    (1, 0, 64, True, False),
    (0, 0, 32, False, False), (0, 32, 32, False, False),
    (4, 0, 16, False, False),
)
A, O, C, G, DM, DU, DB, DQKV = range(8)


def nt(left, right):
    return lax.dot_general(left, right, (((1,), (1,)), ((), ())), preferred_element_type=F)


def tn(left, right):
    return lax.dot_general(left, right, (((0,), (0,)), ((), ())), preferred_element_type=F)


def nn(left, right):
    return jnp.dot(left, right, preferred_element_type=F)


def tiles(total, step):
    def run(body):
        @pl.loop(0, total // step)
        def _(i):
            body(pl.ds(pl.multiple_of(i * step, step), step))

    return run


def normed(values):
    centred = values - jnp.mean(values, axis=-1, keepdims=True)
    scale = lax.rsqrt(jnp.mean(centred * centred, axis=-1, keepdims=True) + 1e-6)
    return centred * scale, scale


def norm_into(out, rows, gain, shift):
    @tiles(rows.shape[0], 64)
    def _(r):
        hat, _ = normed(rows[r, :].astype(F))
        out[r, :] = (hat * gain[...] + shift[...]).astype(B)


def norm_back(rows, grad, base, out, gain, gain_sum, shift_sum):
    @tiles(rows.shape[0], 64)
    def _(r):
        hat, scale = normed(rows[r, :].astype(F))
        d = grad[r, :]
        gain_sum[...] += jnp.sum(d * hat, axis=0, keepdims=True)
        shift_sum[...] += jnp.sum(d, axis=0, keepdims=True)
        d = d * gain[...]
        mean = jnp.mean(d, axis=-1, keepdims=True)
        along = jnp.mean(d * hat, axis=-1, keepdims=True)
        out[r, :] = (base[r, :].astype(F) + scale * (d - mean - hat * along)).astype(out.dtype)


def halves(pair):
    low = lax.broadcasted_iota(jnp.int32, pair.shape, 1) < HEAD
    zero = jnp.zeros_like(pair)
    return jnp.where(low, pair, zero), jnp.where(low, zero, pair)


def head_pairs(qkv, group, many):
    width = qkv.shape[1] // 3
    for i in range(many):
        for t in range(qkv.shape[0] // 128):
            cols = [pl.ds(pl.multiple_of(g * width + (group * many + i) * 128, 128), 128) for g in range(3)]
            yield pl.ds(t * 128, 128), cols


def softmaxes(items, bias):
    scores = [nt(qh, k) + bias[r, :] for r, q, k in items for qh in halves(q)]
    peaks = [jnp.max(s, axis=-1, keepdims=True) for s in scores]
    raised = [jnp.exp(s - m) for s, m in zip(scores, peaks)]
    totals = [1.0 / jnp.sum(e, axis=-1, keepdims=True) for e in raised]
    return [e * t for e, t in zip(raised, totals)]


def attend(qkv, mixed, bias):
    many = 1024 // qkv.shape[0]

    @pl.loop(0, qkv.shape[1] // 384 // many)
    def _(group):
        where = list(head_pairs(qkv, group, many))
        q, k, v = ([qkv[r, cols[g]] for r, cols in where] for g in range(3))
        q = [item * jnp.asarray(HEAD**-0.5, B) for item in q]
        probs = [p.astype(B) for p in softmaxes([(r, a, b) for (r, _), a, b in zip(where, q, k)], bias)]
        for n, (r, cols) in enumerate(where):
            low, high = halves(v[n])
            mixed[r, cols[0]] = (nn(probs[2 * n], low) + nn(probs[2 * n + 1], high)).astype(B)


def attend_back(qkv, grad, bias):
    many = 1024 // qkv.shape[0]

    def joined(items, axis):
        return jnp.concatenate(items, axis)

    @pl.loop(0, qkv.shape[1] // 384 // many)
    def _(group):
        where = list(head_pairs(qkv, group, many))
        q, k, v = ([qkv[r, cols[g]] for r, cols in where] for g in range(3))
        q = [item * jnp.asarray(HEAD**-0.5, B) for item in q]
        d = [grad[r, cols[0]] for r, cols in where]
        probs = softmaxes([(r, a, b) for (r, _), a, b in zip(where, q, k)], bias)
        slopes = [nt(dh, v[n]) for n in range(len(where)) for dh in halves(d[n])]
        centres = [jnp.sum(g * p, axis=-1, keepdims=True) for g, p in zip(slopes, probs)]
        slopes = [(p * (g - c)).astype(B) for p, g, c in zip(probs, slopes, centres)]
        probs = [p.astype(B) for p in probs]
        for n, (r, cols) in enumerate(where):
            pair = slice(2 * n, 2 * n + 2)
            grad_q = nn(joined(slopes[pair], 1), joined(halves(k[n]), 0))
            qkv[r, cols[0]] = (grad_q * HEAD**-0.5).astype(B)
            qkv[r, cols[1]] = tn(joined(slopes[pair], 0), joined(halves(q[n]), 0)).astype(B)
            qkv[r, cols[2]] = tn(joined(probs[pair], 0), joined(halves(d[n]), 0)).astype(B)


def relay(names, *refs):
    ref = dict(zip(names, refs))
    width = ref["x_own"].shape[1]
    rows = ref["x_own"].shape[0]
    ff = ref["w2"].shape[1]
    shard = [ref[f"own{j}"] for j in range(5)]
    full = [ref[f"w{j}"] for j in range(5)]
    both = [ref[n] for n in ("a", "o", "c", "g", "dm", "du", "db", "dqkv")]
    mine = [b.at[pl.ds(0, 2 * rows)] for b in both]
    theirs = [b.at[pl.ds(2 * rows, 2 * rows)] for b in both]
    vec = {n: ref["v_" + n] for n in VECTORS}
    vsum = {n: ref["d_" + n] for n in VECTORS}
    x, hidden, wide, dmixed, result = (ref[n] for n in ("x", "h", "wide", "do", "y"))
    for name in ("g1", "s1", "g2", "s2"):
        vsum[name][...] = jnp.zeros_like(vsum[name])
    p = lax.axis_index("dp")
    z, y, core = p // 4, (p // 2) % 2, p % 2
    inner = jnp.logical_or(z == 1, z == 2)
    section = lax.axis_index("section")
    zo, zn = jnp.where(z == 1, 0, 3), 3 - z
    zon = 3 - zo
    zi = jnp.where(z == 0, 1, 2)

    def idx(z, y, core):
        return (z * 2 + y) * 2 + core

    sibling, across, other = idx(z, y, 1 - core), idx(z, 1 - y, core), idx(zn, y, core)
    outer_one, inner_one = idx(zo, y, core), idx(zi, y, core)

    def remote(sec, src, dst, send_sem, recv_sem, to):
        return pltpu.make_async_remote_copy(
            src_ref=src, dst_ref=dst, send_sem=send_sem, recv_sem=recv_sem,
            device_id=(sec, to), device_id_type=MESH,
        )

    first = section == 0

    def only(condition):
        return lambda body: pl.when(condition)(body)

    class Flow:
        def __init__(self):
            self.sent = []

        def send(self, src, dst, made, recv_sem, to, sec=section):
            remote(sec, src, dst, made()[1], recv_sem, to).start()
            self.note(made)

        def note(self, made, condition=None):
            self.sent.append((made, condition))

        def arrived(self, dst, recv_sem):
            remote(section, dst, dst, ref["idle_sem"].at[0], recv_sem, sibling).wait_recv()

        def finish(self):
            for made, condition in self.sent:
                def wait():
                    like, send_sem = made()
                    remote(section, like, like, send_sem, ref["idle_sem"].at[0], sibling).wait_send()

                wait() if condition is None else pl.when(condition)(wait)
            self.sent = []

    def piece(k, b):
        j, first, count = PARTS[k][:3]
        size = shard[j].shape[0]
        return full[j].at[pl.ds(pl.multiple_of(b * size + first, count), count)]

    def own_piece(k):
        j, first, count = PARTS[k][:3]
        return shard[j].at[pl.ds(first, count)]

    def own_copy(k):
        return pltpu.make_async_copy(own_piece(k), piece(k, p), ref["ag_local"].at[k])

    def gather_steps(flow, is_inner):
        used = [0] * len(PARTS)

        def send(k, b, to, own=False):
            src = own_piece(k) if own else piece(k, b)
            n = used[k]

            def made():
                return full[PARTS[k][0]].at[pl.ds(0, PARTS[k][2])], ref["ag_send"].at[k, n]

            flow.send(src, piece(k, b), made, ref["ag_recv"].at[k, b], to)
            used[k] += 1

        def take(k, b, *to):
            flow.arrived(piece(k, b), ref["ag_recv"].at[k, b])
            for target in to:
                send(k, b, target)

        def begin(k):
            if is_inner:
                for to in (outer_one if PARTS[k][4] else across, other, sibling):
                    send(k, p, to, own=True)
                own_copy(k).start()
            else:
                send(k, p, inner_one, own=True)
                send(k, p, across, own=True)

        def early(k):
            take(k, idx(zo, y, core), other, sibling)
            take(k, idx(zn, y, core), across, sibling)
            if not PARTS[k][4]:
                take(k, idx(z, 1 - y, core), sibling)

        def late(k):
            by_z = PARTS[k][3]
            take(k, idx(zon, y, core), *((sibling,) if by_z else (across, sibling)))
            take(k, idx(zo, 1 - y, core), *((other, sibling) if by_z else (sibling,)))

        def end(k):
            if PARTS[k][4]:
                take(k, idx(z, 1 - y, core), sibling)
            take(k, idx(zn, 1 - y, core), sibling)
            take(k, idx(zon, 1 - y, core), sibling)

        def step(k):
            if k == 0:
                for first in range(AHEAD):
                    begin(first)
            if k + AHEAD < len(PARTS):
                begin(k + AHEAD)
            if is_inner:
                for stage, n in ((early, k), (late, k - 1), (end, k - 2)):
                    if 0 <= n < len(PARTS):
                        stage(n)
            else:
                take(k, across, inner_one)
                if PARTS[k][4]:
                    take(k, idx(zi, y, core), across)
                if k and PARTS[k - 1][4]:
                    take(k - 1, idx(zi, 1 - y, core), inner_one)

        return step

    def gathered(flow, j):
        for k, part in enumerate(PARTS):
            if part[0] == j:
                own_copy(k).wait()
                for b in range(8):
                    block = 2 * b + 1 - core
                    flow.arrived(piece(k, block), ref["ag_recv"].at[k, block])

    def write_small():
        stage = ref["stage"]
        stage[...] = jnp.zeros_like(stage)
        for c in range(2):
            @pl.when(core == c)
            def _():
                for n, name in enumerate(VECTORS[:6]):
                    stage[n : n + 1, 64 * c : 64 * c + 64] = ref["in_" + name][...].astype(F)
        for n in range(2):
            stage[6 + n : 7 + n, :] = ref["in_bu"][:, 128 * n : 128 * n + 128].astype(F)
        shard[4][...] = stage[...].astype(B)

    def write_crops():
        for m in range(2):
            ref["crops"][0:1, 64 * m : 64 * m + 64] = (ref["in_crop"][m : m + 1, :] + 1024 * m).astype(F)

    def write_bias(crops, first):
        along = jnp.broadcast_to(crops[0:1, :], (rows, rows))
        ref["bias"][pl.ds(first, rows), :] = jnp.where(along == along.T, 0.0, -1e30)

    def spread_vectors():
        for i in range(8):
            low = full[4][pl.ds(32 * i, 16), :].astype(F)
            high = full[4][pl.ds(32 * i + 16, 16), :].astype(F)
            joined = low + high
            for n, name in enumerate(VECTORS[:6]):
                vec[name][:, pl.ds(128 * i, 128)] = joined[n : n + 1]
            for n, part in enumerate((low[6:7], low[7:8], high[6:7], high[7:8])):
                vec["bu"][:, pl.ds(512 * i + 128 * n, 128)] = part

    def exchange(flow, which):
        pair = ref["act_send"].at[which], ref["act_recv"].at[which]
        remote(section, mine[which], theirs[which], *pair, sibling).start()

    def exchanged(flow, *which):
        for w in which:
            flow.arrived(theirs[w], ref["act_recv"].at[w])

    def forward_attend(r):
        norm_into(mine[A].at[r], x.at[r], vec["g1"], vec["s1"])

        @tiles(3 * width, 1536)
        def _(c):
            mine[DQKV][r, c] = nn(mine[A][r, :], full[0][:, c]).astype(B)

        attend(mine[DQKV].at[r], mine[O].at[r], ref["bias"].at[r])

    def forward_out(r):
        hidden[r, :] = x[r, :].astype(F) + nn(mine[O][r, :], full[1][...]) + vec["bo"][...]
        norm_into(mine[C].at[r], hidden.at[r], vec["g2"], vec["s2"])

    def forward_up(r):
        @tiles(ff, 1024)
        def _(c):
            u = nn(mine[C][r, :], full[2][:, c]) + vec["bu"][:, c]
            phi = 0.5 + 0.5 * lax.erf(u * 0.5**0.5)
            mine[G][r, c] = (u * phi).astype(B)
            mine[DU][r, c] = (phi + u * (jnp.exp(-0.5 * u * u) * (0.5 / jnp.pi) ** 0.5)).astype(B)

    def forward_down(r):
        result[r, :] = (hidden[r, :] + nn(mine[G][r, :], full[3][...]) + vec["bd"][...]).astype(B)

    def backward_du():
        vsum["bd"][...] = jnp.sum(mine[DM][...].astype(F), axis=0, keepdims=True)

        @tiles(ff, 1024)
        def _(c):
            du = (nt(mine[DM][...], full[3][c, :]) * mine[DU][:, c].astype(F)).astype(B)
            mine[DU][:, c] = du
            vsum["bu"][:, c] = jnp.sum(du.astype(F), axis=0, keepdims=True)

    def backward_dh():
        wide[...] = nt(mine[DU][...], full[2][...])
        norm_back(hidden, wide, mine[DM], hidden, vec["g2"], vsum["g2"], vsum["s2"])
        mine[DB][...] = hidden[...].astype(B)
        vsum["bo"][...] = jnp.sum(mine[DB][...].astype(F), axis=0, keepdims=True)

    def backward_attend():
        dmixed[...] = nt(mine[DB][...], full[1][...]).astype(B)
        attend_back(mine[DQKV], dmixed, ref["bias"])

    def backward_da():
        wide[...] = nt(mine[DQKV][...], full[0][...])

    def backward_dx(r):
        norm_back(x.at[r], wide.at[r], hidden.at[r], x.at[r], vec["g1"], vsum["g1"], vsum["s1"])

    def packed(which):
        src, out = both[which], ref["packed"]
        for i in range(width // 256):
            first = src[:, pl.ds(256 * i, 128)].astype(F)
            second = src[:, pl.ds(256 * i + 128, 128)].astype(F)
            low = lax.broadcasted_iota(jnp.int32, first.shape, 1) < HEAD
            even = jnp.where(low, first, pltpu.roll(second, HEAD, 1))
            odd = jnp.where(low, pltpu.roll(first, HEAD, 1), second)
            out[pl.ds(128 * i, 128), :] = jnp.where(core == 0, even, odd).T.astype(B)

    def grad_down():
        size = shard[3].shape[0]
        for o in range(8):
            c = pl.ds(pl.multiple_of(size * (2 * o + core), size), size)
            full[3][pl.ds(size * o, size), :] = tn(both[G][:, c], both[DM][...]).astype(B)

    def grad_of(j, left, right):
        packed(left)

        @tiles(both[right].shape[1], 512)
        def _(c):
            full[j][pl.ds(0, 8 * shard[j].shape[0]), c] = nn(ref["packed"][...], both[right][:, c]).astype(B)

    def grad_vectors():
        for o in range(8):
            for n, name in enumerate(VECTORS[:6]):
                ref["vp"][pl.ds(16 * o + n, 1), :] = vsum[name][:, pl.ds(128 * o, 128)]
            for n in range(4):
                ref["vp"][pl.ds(16 * o + 6 + n, 1), :] = vsum["bu"][:, pl.ds(512 * o + 128 * n, 128)]
            ref["vp"][pl.ds(16 * o + 10, 6), :] = jnp.zeros((6, 128), F)

    partial = [full[0], full[1], full[2], full[3], ref["vp"]]
    sums = [ref[f"out{j}"] for j in range(4)] + [ref["vs"]]
    NEAR, OWN, ALT, INNER, OUTER = range(5)
    slots = [[ref[f"r{s}_{j}"] for j in range(5)] for s in range(5)]

    def reducer(flow):
        def slot(s, k):
            j, first, count = SUMS[k][:3]
            return slots[s][j].at[pl.ds(first, count)]

        def part(k, zz, yy):
            j, first, count = SUMS[k][:3]
            size = partial[j].shape[0] // 8 if j == 4 else shard[j].shape[0]
            return partial[j].at[pl.ds(pl.multiple_of((zz * 2 + yy) * size + first, count), count)]

        def send(k, n, src, s, to):
            def made():
                return slot(s, k), ref["rs_send"].at[k, n]

            flow.send(src, slot(s, k), made, ref["rs_recv"].at[k, s], to)

        def arrived(k, s):
            flow.arrived(slot(s, k), ref["rs_recv"].at[k, s])

        def add(k, dst, *more):
            total = dst[...].astype(F)
            for s in more:
                total = total + slot(s, k)[...].astype(F)
            return total

        def issue(k):
            if SUMS[k][3]:
                send(k, 4, part(k, zon, y), OUTER, other)
                send(k, 1, part(k, zon, 1 - y), ALT, other)
            else:
                send(k, 1, part(k, zon, 1 - y), ALT, across)
                send(k, 6, part(k, zo, 1 - y), INNER, outer_one)

        def issue_near(k):
            send(k, 0, part(k, zn, 1 - y), NEAR, across)

        def issue_own(k):
            if SUMS[k][4]:
                send(k, 2, part(k, z, 1 - y), NEAR, outer_one)
            else:
                send(k, 2, part(k, z, 1 - y), OWN, across)

        def far_on(k):
            if not SUMS[k][3]:
                dst = part(k, zon, y)
                arrived(k, ALT)
                dst[...] = add(k, dst, ALT).astype(dst.dtype)
                send(k, 4, dst, OUTER, other)

        def near_on(k):
            dst = part(k, zn, y)
            arrived(k, NEAR)
            dst[...] = add(k, dst, NEAR).astype(dst.dtype)
            send(k, 3, dst, INNER, other)

        def outward(k):
            dst = part(k, zo, y)
            arrived(k, OUTER)
            dst[...] = add(k, dst, OUTER).astype(dst.dtype)
            send(k, 5, dst, OUTER, outer_one)
            if SUMS[k][3]:
                dst = part(k, zo, 1 - y)
                arrived(k, ALT)
                dst[...] = add(k, dst, ALT).astype(dst.dtype)
                send(k, 6, dst, INNER, outer_one)

        def last(k):
            arrived(k, INNER)
            arrived(k, OWN)
            j, first, count = SUMS[k][:3]
            sums[j][pl.ds(first, count), :] = add(k, part(k, z, y), OWN, INNER)

        def pass_on(k):
            arrived(k, INNER)
            send(k, 0, slot(INNER, k), OWN, across)

        def around(k, end):
            arrived(k, ALT if end else NEAR)
            if end:
                send(k, 2, slot(ALT, k), OWN, inner_one)
            else:
                send(k, 1, slot(NEAR, k), ALT, across)

        def collect(k):
            arrived(k, OUTER)
            arrived(k, OWN)
            j, first, count = SUMS[k][:3]
            sums[j][pl.ds(first, count), :] = slot(OUTER, k)[...].astype(F) + slot(OWN, k)[...].astype(F)

        def join_vectors():
            made = lambda: (ref["vs"], ref["vec_sem"].at[0])
            flow.send(ref["vs"], ref["vt"], made, ref["vec_sem"].at[1], sibling)
            flow.arrived(ref["vt"], ref["vec_sem"].at[1])
            ref["out4"][...] = ref["vs"][...] + ref["vt"][...]

        inner_steps = issue, issue_near, issue_own, far_on, near_on, outward, last
        return inner_steps, (pass_on, around, collect), join_vectors

    def hand_out(flow, src, out, n):
        made = lambda: (out, ref["res_send"].at[n])
        flow.send(src.at[pl.ds(rows, rows)], out, made, ref["res_recv"].at[n], outer_one)
        out[...] = src[pl.ds(0, rows), :]

    every = pl.ds(0, 2 * rows)
    near, far = pl.ds(0, rows), pl.ds(rows, rows)

    def half(h):
        return pl.ds(pl.multiple_of(h * rows, rows), rows)

    def inner_program():
        flow = Flow()
        step = gather_steps(flow, True)
        inner_steps, _, join_vectors = reducer(flow)
        issue, issue_near, issue_own, far_on, near_on, outward, last = inner_steps
        step(0)
        own = [
            pltpu.make_async_copy(src, dst.at[near], ref["tok_local"].at[0])
            for src, dst in ((ref["x_own"], x), (ref["dy_own"], mine[DM]))
        ]
        for n, copy in enumerate(own):
            pl.when(section == n)(copy.start)
        write_bias(ref["crops"], 0)

        def tokens():
            for n, (copy, dst) in enumerate(zip(own, (x, mine[DM]))):
                @pl.when(section == n)
                def _():
                    copy.wait()
                    flow.arrived(dst.at[far], ref["tok_recv"].at[1])
            flow.arrived(ref["far_crops"], ref["tok_recv"].at[0])
            write_bias(ref["far_crops"], rows)

        def steps(begin, end):
            for k in range(begin, end):
                step(k)

        @pl.loop(0, 2)
        def _(turn):
            gathering, active = only(turn == 0), only(section == turn)

            @gathering
            def _():
                steps(1, 6)
                gathered(flow, 4)
                spread_vectors()
                tokens()
                gathered(flow, 0)

            @active
            def _():
                @pl.loop(0, 2)
                def _(h):
                    @pl.when(jnp.logical_not(first))
                    def _():
                        flow.arrived(x.at[half(h)], ref["x_recv"].at[h])

                    forward_attend(half(h))

            @gathering
            def _():
                steps(6, 7)
                gathered(flow, 1)

            @active
            def _():
                forward_out(every)

            @gathering
            def _():
                steps(7, 9)
                gathered(flow, 2)

            @active
            def _():
                forward_up(every)

            @gathering
            def _():
                steps(9, len(PARTS) + 2)
                gathered(flow, 3)

            @active
            def _():
                forward_down(every)

        @pl.when(first)
        def _():
            for n, r in enumerate((near, far)):
                remote(1, result.at[r], x.at[r], ref["x_send"].at[n], ref["x_recv"].at[n], p).start()

        for n in range(2):
            flow.note(lambda n=n: (result.at[near], ref["x_send"].at[n]), first)
        flow.finish()
        for which in (G, C, O, A):
            exchange(flow, which)
        hand_out(flow, result, ref["y_out"], 0)

        def exchange_when(condition, *which):
            @pl.when(condition)
            def _():
                for w in which:
                    exchange(flow, w)

        @pl.loop(0, 2)
        def _(turn):
            main, grads = only(turn == 0), only(section == turn)
            leading = jnp.logical_and(turn == 0, first)
            trailing = jnp.logical_and(turn == 1, section == 1)

            @pl.when(leading)
            def _():
                for n, r in enumerate((near, far)):
                    flow.arrived(mine[DM].at[r], ref["x_recv"].at[2 + n])

            exchange_when(turn == 0, DM)
            main(backward_du)
            exchange_when(leading, DU)
            exchange_when(trailing, DU, DB, DQKV)

            @grads
            def _():
                exchanged(flow, G, DM)
                grad_down()
                issue(0)
                issue_near(0)

            main(backward_dh)
            exchange_when(leading, DB)

            @grads
            def _():
                issue(1)
                issue_near(1)
                exchanged(flow, C, DU)
                grad_of(2, C, DU)

            main(backward_attend)
            exchange_when(leading, DQKV)

            @grads
            def _():
                issue(2)
                issue(3)
                issue_near(2)
                exchanged(flow, O, DB)
                grad_of(1, O, DB)
                issue(4)

            main(backward_da)

            @grads
            def _():
                far_on(1)
                near_on(0)
                exchanged(flow, A, DQKV)
                grad_of(0, A, DQKV)
                issue(5)
                issue(6)
                issue_near(3)

            @main
            def _():
                @pl.loop(0, 2)
                def _(h):
                    r = half(h)
                    backward_dx(r)

                    @pl.when(jnp.logical_not(first))
                    def _():
                        to = mine[DM].at[r]
                        remote(0, x.at[r], to, ref["x_send"].at[2 + h], ref["x_recv"].at[2 + h], p).start()

        for n in range(2):
            flow.note(lambda n=n: (x.at[near], ref["x_send"].at[2 + n]), jnp.logical_not(first))
        for which in range(8):
            flow.note(lambda w=which: (mine[w], ref["act_send"].at[w]))
        grad_vectors()
        issue(7)
        hand_out(flow, x, ref["dx_out"], 1)
        count = len(SUMS)
        for k in range(2, count + 3):
            for turn, n in ((far_on, k), (issue_near, k + 2), (near_on, k - 1), (outward, k - 2), (issue_own, k - 3)):
                if 0 <= n < count:
                    turn(n)
        for k in range(count):
            last(k)
        join_vectors()
        flow.finish()

    def outer_program():
        flow = Flow()
        step = gather_steps(flow, False)
        _, (pass_on, around, collect), join_vectors = reducer(flow)
        for k in range(len(PARTS)):
            step(k)
            if k == 1:
                made = lambda: (ref["crops"], ref["tok_send"].at[0])
                flow.send(ref["crops"], ref["far_crops"], made, ref["tok_recv"].at[0], inner_one)
                for n, (src, dst) in enumerate(((ref["x_own"], x), (ref["dy_own"], mine[DM]))):
                    pl.when(section == n)(
                        remote(section, src, dst.at[far], ref["tok_send"].at[1], ref["tok_recv"].at[1], inner_one).start
                    )
                flow.note(lambda: (x.at[far], ref["tok_send"].at[1]))
        for k in range(len(SUMS) + 3):
            for turn, n in ((pass_on, k), (collect, k - 1)):
                if 0 <= n < len(SUMS) and (k < len(SUMS) or turn is pass_on):
                    turn(n)
            for end in range(2):
                n = k - 3 - end
                if 0 <= n < len(SUMS) and SUMS[n][4]:
                    around(n, end)
        collect(len(SUMS) - 1)
        join_vectors()
        flow.arrived(ref["y_out"], ref["res_recv"].at[0])
        flow.arrived(ref["dx_out"], ref["res_recv"].at[1])
        flow.finish()

    write_small()
    write_crops()
    pl.when(inner)(inner_program)
    pl.when(jnp.logical_not(inner))(outer_program)


def relay_call(x_own, dy_own, small, shards, dp):
    rows, width = x_own.shape
    ff = shards[2].shape[1]
    count = 2 * rows
    shapes = [item.shape for item in shards] + [(16, 128)]
    inputs = {"x_own": x_own, "dy_own": dy_own}
    inputs.update({f"own{j}": item for j, item in enumerate(shards)})
    outputs = {"y_out": ((rows, width), B), "dx_out": ((rows, width), B)}
    outputs.update({f"out{j}": (item.shape, F) for j, item in enumerate(shards)})
    outputs["out4"] = ((16, 128), F)
    scratch = {f"w{j}": ((dp * shape[0], shape[1]), B) for j, shape in enumerate(shapes)}
    for name, cols in zip(("a", "o", "c", "g", "dm", "du", "db", "dqkv"), (1, 1, 1, 0, 1, 0, 1, 3)):
        scratch[name] = ((2 * count, cols * width or ff), B)
    scratch.update(x=((count, width), B), h=((count, width), F), wide=((count, width), F), do=((count, width), B))
    scratch.update(y=((count, width), B), bias=((count, 128), F), packed=((width // 2, 2 * count), B))
    for name in VECTORS:
        scratch["v_" + name] = scratch["d_" + name] = ((1, ff if name == "bu" else width), F)
    scratch.update(vp=((128, 128), F), vs=((16, 128), F), vt=((16, 128), F), stage=((16, 128), F), crops=((8, 128), F), far_crops=((8, 128), F), own4=((16, 128), B))
    for s in range(5):
        for j, shape in enumerate(shapes):
            scratch[f"r{s}_{j}"] = (shape, F if j == 4 else B)
    sems = dict(
        ag_send=(len(PARTS), 16), ag_recv=(len(PARTS), dp), ag_local=(len(PARTS),), tok_local=(1,), tok_send=(2,),
        tok_recv=(2,), x_send=(4,), x_recv=(4,), act_send=(8,), act_recv=(8,), res_send=(2,), res_recv=(2,),
        rs_send=(len(SUMS), 7), rs_recv=(len(SUMS), 5), vec_sem=(2,), idle_sem=(1,),
    )
    names = [*inputs, *small, *outputs, *scratch, *sems]
    whole, anywhere = pl.BlockSpec(memory_space=pltpu.VMEM), pl.BlockSpec(memory_space=pl.ANY)
    return pl.pallas_call(
        functools.partial(relay, names),
        out_shape=[jax.ShapeDtypeStruct(*item) for item in outputs.values()],
        in_specs=[anywhere] * len(inputs) + [whole] * len(small),
        out_specs=[whole] * len(outputs),
        scratch_shapes=[pltpu.VMEM(*item) for item in scratch.values()]
        + [pltpu.SemaphoreType.DMA(item) for item in sems.values()],
        compiler_params=pltpu.CompilerParams(has_side_effects=True, vmem_limit_bytes=62 << 20),
        name="relay",
    )(*inputs.values(), *small.values())


def hand_over(*refs):
    rows, vectors, out, small = refs[:6], refs[6], refs[7:13], refs[13:20]
    for n in range(2):
        size = out[n].shape[2]
        for m in range(out[n].shape[1]):
            out[n][0, m] = rows[n][pl.ds(m * size, size), :]
    for n in range(2, 6):
        out[n][0] = rows[n][...]
    core = lax.axis_index("dp") % 2
    for c in range(2):
        @pl.when(core == c)
        def _():
            for n in range(6):
                small[n][...] = vectors[n : n + 1, 64 * c : 64 * c + 64]
            small[6][...] = vectors[6 + 2 * c : 8 + 2 * c, :]


def middle(
    block_input, crop_ids, out_grad, norm1_gain, norm1_shift, w_qkv, w_out, b_out,
    norm2_gain, norm2_shift, w_up, b_up, w_down, b_down,
):
    micro, rows, width = block_input.shape
    small = dict(zip(VECTORS, (norm1_gain, norm1_shift, b_out, norm2_gain, norm2_shift, b_down, b_up)))
    small = {"in_" + name: item for name, item in small.items()} | {"in_crop": crop_ids}
    got = relay_call(
        block_input.reshape(-1, width), out_grad.reshape(-1, width), small,
        (w_qkv[0], w_out[0], w_up[0], w_down[0]), lax.axis_size("dp"),
    )
    whole = pl.BlockSpec(memory_space=pltpu.VMEM)
    shapes = [((1, micro, rows, width), B)] * 2 + [((1,) + item.shape, F) for item in got[2:6]]
    shapes += [((1, 64), F)] * 6 + [((2, 128), F)]
    y, dx, g_qkv, g_out, g_up, g_down, g1, s1, bo, g2, s2, bd, bu = pl.pallas_call(
        hand_over,
        out_shape=[jax.ShapeDtypeStruct(*item) for item in shapes],
        in_specs=[whole] * 7,
        out_specs=[whole] * 13,
        compiler_params=pltpu.CompilerParams(vmem_limit_bytes=62 << 20),
        name="hand_over",
    )(*got)
    return y, dx, g1, s1, g_qkv, g_out, bo, g2, s2, g_up, bu.reshape(1, -1), g_down, bd


def solution(mesh):
    in_specs = (
        P(None, "dp", None),
        P(None, "dp"),
        P(None, "dp", None),
        P("section", "dp"),
        P("section", "dp"),
        P("section", "dp", None),
        P("section", "dp", None),
        P("section", "dp"),
        P("section", "dp"),
        P("section", "dp"),
        P("section", "dp", None),
        P("section", "dp"),
        P("section", "dp", None),
        P("section", "dp"),
    )
    out_specs = (
        P("section", None, "dp", None),
        P("section", None, "dp", None),
        P("section", "dp"),
        P("section", "dp"),
        P("section", "dp", None),
        P("section", "dp", None),
        P("section", "dp"),
        P("section", "dp"),
        P("section", "dp"),
        P("section", "dp", None),
        P("section", "dp"),
        P("section", "dp", None),
        P("section", "dp"),
    )
    fits = mesh.shape["dp"] == 16 and mesh.shape["section"] == 2
    return jax.shard_map(middle if fits else local, mesh=mesh, in_specs=in_specs, out_specs=out_specs, check_vma=False)
```

profile of v0, /device:TPU:0, one launch (start us, length us, event | category | flops | bytes accessed | tf_op | source)
XLA Modules:
  0.0 268.9 jit_solution(9871278253193842176)
XLA Ops:
  0.7 264.0 %relay.1 = (bf16[128,1024]{1,0:T(8,128)(2,1)}, bf16[128,1024]{1,0:T(8,128)(2,1)}, f32[64,3072]{1,0:T(8,128)}, f32[64,1024]{1,0:T(8,128)}, f32[64,4096]{1,0:T(8,1...) custom-call(bf16[128,1024]{1,0:T(8,128)(2,1)} %bitcast.10, bf16[128,1024]{1,0:T(8,128)(2,1)} %bitcast.11, ...), custom_call_target="tpu_custom_call" | custom-call | tf_op jit(solution)/shard_map/relay/pallas_call | solution.py:1053
  264.6 4.1 %hand_over.1 = (bf16[1,2,64,1024]{3,2,1,0:T(8,128)(2,1)}, bf16[1,2,64,1024]{3,2,1,0:T(8,128)(2,1)}, f32[1,64,3072]{2,1,0:T(8,128)}, f32[1,64,1024]{2,1,0:T(8,128...) custom-call(bf16[128,1024]{1,0:T(8,128)(2,1)} %get-tuple-element.33., ...), custom_call_target="tpu_custom_call" | custom-call | tf_op jit(solution)/shard_map/hand_over/pallas_call | solution.py:1096
where the time goes:
time: 269 us
  Pallas kernels  268 us (100%)
    pallas_call x1, Pallas kernels, relay_call(): pl.pallas_call(functools.partial(relay, names), out_shape=[jax.ShapeDtype...  264 us

commit v1 on v0

--- a/solution.py
+++ b/solution.py
@@ -309,14 +309,21 @@
     (0, 0, 32, False, False), (0, 32, 32, False, False),
     (1, 0, 64, True, False),
     (2, 0, 32, False, True), (2, 32, 32, True, False),
-    (3, 0, 128, False, False), (3, 128, 128, True, False),
+    (3, 0, 64, False, False), (3, 64, 64, True, False), (3, 128, 64, False, False), (3, 192, 64, True, False),
 )
 AHEAD = 4
 SUMS = (
-    (3, 0, 128, True, False), (3, 128, 128, False, True),
-    (2, 0, 32, True, False), (2, 32, 32, False, False),
-    (1, 0, 64, True, False),
-    (0, 0, 32, False, False), (0, 32, 32, False, False),
+    (3, 0, 64, True, False),
+    (3, 64, 64, False, False),
+    (3, 128, 64, True, False),
+    (3, 192, 64, False, False),
+    (2, 0, 16, True, False),
+    (2, 16, 16, False, False),
+    (2, 32, 16, True, False),
+    (2, 48, 16, False, False),
+    (1, 0, 64, False, False),
+    (0, 0, 32, True, False),
+    (0, 32, 32, False, False),
     (4, 0, 16, False, False),
 )
 A, O, C, G, DM, DU, DB, DQKV = range(8)
@@ -924,14 +931,17 @@
                 grad_down()
                 issue(0)
                 issue_near(0)
+                issue(1)
+                issue_near(1)
 
             main(backward_dh)
             exchange_when(leading, DB)
 
             @grads
             def _():
-                issue(1)
-                issue_near(1)
+                issue(2)
+                issue_near(2)
+                issue(3)
                 exchanged(flow, C, DU)
                 grad_of(2, C, DU)
 
@@ -940,12 +950,12 @@
 
             @grads
             def _():
-                issue(2)
-                issue(3)
-                issue_near(2)
+                for k in range(4, 8):
+                    issue(k)
+                issue_near(3)
                 exchanged(flow, O, DB)
                 grad_of(1, O, DB)
-                issue(4)
+                issue(8)
 
             main(backward_da)
 
@@ -955,9 +965,9 @@
                 near_on(0)
                 exchanged(flow, A, DQKV)
                 grad_of(0, A, DQKV)
-                issue(5)
-                issue(6)
-                issue_near(3)
+                issue(9)
+                issue(10)
+                issue_near(4)
 
             @main
             def _():
@@ -976,13 +986,15 @@
         for which in range(8):
             flow.note(lambda w=which: (mine[w], ref["act_send"].at[w]))
         grad_vectors()
-        issue(7)
+        issue(11)
         hand_out(flow, x, ref["dx_out"], 1)
         count = len(SUMS)
-        for k in range(2, count + 3):
-            for turn, n in ((far_on, k), (issue_near, k + 2), (near_on, k - 1), (outward, k - 2), (issue_own, k - 3)):
-                if 0 <= n < count:
-                    turn(n)
+        for k in range(2, count + 4):
+            plan = ((far_on, [2 * k - 2, 2 * k - 1]), (issue_near, [k + 3]), (near_on, [k - 1]), (outward, [k - 3] if k < 8 else [2 * k - 11, 2 * k - 10]), (issue_own, [k - 4]))
+            for turn, which in plan:
+                for n in which:
+                    if 0 <= n < count:
+                        turn(n)
         for k in range(count):
             last(k)
         join_vectors()
@@ -1002,9 +1014,9 @@
                         remote(section, src, dst.at[far], ref["tok_send"].at[1], ref["tok_recv"].at[1], inner_one).start
                     )
                 flow.note(lambda: (x.at[far], ref["tok_send"].at[1]))
-        for k in range(len(SUMS) + 3):
+        for k in range(len(SUMS)):
             for turn, n in ((pass_on, k), (collect, k - 1)):
-                if 0 <= n < len(SUMS) and (k < len(SUMS) or turn is pass_on):
+                if 0 <= n:
                     turn(n)
             for end in range(2):
                 n = k - 3 - end

time: 269 us -> 262 us (0.974)
  Pallas kernels: 268 us -> 261 us
    pallas_call x1, Pallas kernels: 264 us -> 257 us  [relay_call(): pl.pallas_call(functools.partial(relay, names), out_shape=[jax.ShapeDtype...]
where the time goes in v1:
time: 262 us
  Pallas kernels  261 us (100%)
    pallas_call x1, Pallas kernels, relay_call(): pl.pallas_call(functools.partial(relay, names), out_shape=[jax.ShapeDtype...  257 us

profile of v1, /device:TPU:0, one launch (start us, length us, event | category | flops | bytes accessed | tf_op | source)
XLA Modules:
  0.0 261.9 jit_solution(16303809853033902248)
XLA Ops:
  0.7 256.9 %relay.1 = (bf16[128,1024]{1,0:T(8,128)(2,1)}, bf16[128,1024]{1,0:T(8,128)(2,1)}, f32[64,3072]{1,0:T(8,128)}, f32[64,1024]{1,0:T(8,128)}, f32[64,4096]{1,0:T(8,1...) custom-call(bf16[128,1024]{1,0:T(8,128)(2,1)} %bitcast.10, bf16[128,1024]{1,0:T(8,128)(2,1)} %bitcast.11, ...), custom_call_target="tpu_custom_call" | custom-call | tf_op jit(solution)/shard_map/relay/pallas_call | solution.py:1065
  257.6 4.1 %hand_over.1 = (bf16[1,2,64,1024]{3,2,1,0:T(8,128)(2,1)}, bf16[1,2,64,1024]{3,2,1,0:T(8,128)(2,1)}, f32[1,64,3072]{2,1,0:T(8,128)}, f32[1,64,1024]{2,1,0:T(8,128...) custom-call(bf16[128,1024]{1,0:T(8,128)(2,1)} %get-tuple-element.33., ...), custom_call_target="tpu_custom_call" | custom-call | tf_op jit(solution)/shard_map/hand_over/pallas_call | solution.py:1108

commit v2 on v1

--- a/solution.py
+++ b/solution.py
@@ -815,6 +815,36 @@
     def half(h):
         return pl.ds(pl.multiple_of(h * rows, rows), rows)
 
+    direct = pl.ds(rows, rows // 2)
+    detours = [pl.ds(rows + rows // 4 * n, rows // 4) for n in (2, 3)]
+
+    def cross_far(src, dst, sec, kind, between=lambda: None):
+        for n, r in enumerate(detours):
+            pair = ref["way_send"].at[kind + n], ref["way_recv"].at[kind + n]
+            remote(section, src.at[r], dst.at[r], *pair, outer_one).start()
+        between()
+        pair = ref["x_send"].at[kind + 1], ref["x_recv"].at[kind + 1]
+        remote(sec, src.at[direct], dst.at[direct], *pair, p).start()
+
+    def crossed_far(flow, dst, kind):
+        flow.arrived(dst.at[direct], ref["x_recv"].at[kind + 1])
+        for n, r in enumerate(detours):
+            flow.arrived(dst.at[r], ref["way_recv"].at[kind + n])
+
+    def note_crossing(flow, kind, condition):
+        flow.note(lambda: (x.at[near], ref["x_send"].at[kind]), condition)
+        flow.note(lambda: (x.at[direct], ref["x_send"].at[kind + 1]), condition)
+        for n in range(2):
+            flow.note(lambda n=n: (x.at[detours[0]], ref["way_send"].at[kind + n]), condition)
+
+    def detour(flow, dst, sec, kind):
+        for n, r in enumerate(detours):
+            pair = ref["way_send"].at[kind + n], ref["way_recv"].at[kind + n]
+            flow.arrived(dst.at[r], pair[1])
+            pl.when(section != sec)(remote(sec, dst.at[r], dst.at[r], *pair, p).start)
+            pl.when(section == sec)(remote(sec, dst.at[r], dst.at[r], *pair, inner_one).start)
+            flow.note(lambda n=n: (x.at[detours[0]], ref["way_send"].at[kind + n]))
+
     def inner_program():
         flow = Flow()
         step = gather_steps(flow, True)
@@ -858,9 +888,13 @@
             def _():
                 @pl.loop(0, 2)
                 def _(h):
-                    @pl.when(jnp.logical_not(first))
+                    @pl.when(jnp.logical_and(h == 0, section == 1))
                     def _():
-                        flow.arrived(x.at[half(h)], ref["x_recv"].at[h])
+                        flow.arrived(x.at[near], ref["x_recv"].at[0])
+
+                    @pl.when(jnp.logical_and(h == 1, section == 1))
+                    def _():
+                        crossed_far(flow, x, 0)
 
                     forward_attend(half(h))
 
@@ -893,11 +927,12 @@
 
         @pl.when(first)
         def _():
-            for n, r in enumerate((near, far)):
-                remote(1, result.at[r], x.at[r], ref["x_send"].at[n], ref["x_recv"].at[n], p).start()
-
-        for n in range(2):
-            flow.note(lambda n=n: (result.at[near], ref["x_send"].at[n]), first)
+            cross_far(
+                result, x, 1, 0,
+                remote(1, result.at[near], x.at[near], ref["x_send"].at[0], ref["x_recv"].at[0], p).start,
+            )
+
+        note_crossing(flow, 0, first)
         flow.finish()
         for which in (G, C, O, A):
             exchange(flow, which)
@@ -917,8 +952,8 @@
 
             @pl.when(leading)
             def _():
-                for n, r in enumerate((near, far)):
-                    flow.arrived(mine[DM].at[r], ref["x_recv"].at[2 + n])
+                flow.arrived(mine[DM].at[near], ref["x_recv"].at[2])
+                crossed_far(flow, mine[DM], 2)
 
             exchange_when(turn == 0, DM)
             main(backward_du)
@@ -973,16 +1008,18 @@
             def _():
                 @pl.loop(0, 2)
                 def _(h):
-                    r = half(h)
-                    backward_dx(r)
-
-                    @pl.when(jnp.logical_not(first))
+                    backward_dx(half(1 - h))
+
+                    @pl.when(jnp.logical_and(h == 0, section == 1))
                     def _():
-                        to = mine[DM].at[r]
-                        remote(0, x.at[r], to, ref["x_send"].at[2 + h], ref["x_recv"].at[2 + h], p).start()
-
-        for n in range(2):
-            flow.note(lambda n=n: (x.at[near], ref["x_send"].at[2 + n]), jnp.logical_not(first))
+                        cross_far(x, mine[DM], 0, 2)
+
+                    @pl.when(jnp.logical_and(h == 1, section == 1))
+                    def _():
+                        to = mine[DM].at[near]
+                        remote(0, x.at[near], to, ref["x_send"].at[2], ref["x_recv"].at[2], p).start()
+
+        note_crossing(flow, 2, section == 1)
         for which in range(8):
             flow.note(lambda w=which: (mine[w], ref["act_send"].at[w]))
         grad_vectors()
@@ -1014,6 +1051,8 @@
                         remote(section, src, dst.at[far], ref["tok_send"].at[1], ref["tok_recv"].at[1], inner_one).start
                     )
                 flow.note(lambda: (x.at[far], ref["tok_send"].at[1]))
+        detour(flow, x, 1, 0)
+        detour(flow, mine[DM], 0, 2)
         for k in range(len(SUMS)):
             for turn, n in ((pass_on, k), (collect, k - 1)):
                 if 0 <= n:
@@ -1057,7 +1096,7 @@
             scratch[f"r{s}_{j}"] = (shape, F if j == 4 else B)
     sems = dict(
         ag_send=(len(PARTS), 16), ag_recv=(len(PARTS), dp), ag_local=(len(PARTS),), tok_local=(1,), tok_send=(2,),
-        tok_recv=(2,), x_send=(4,), x_recv=(4,), act_send=(8,), act_recv=(8,), res_send=(2,), res_recv=(2,),
+        tok_recv=(2,), x_send=(4,), x_recv=(4,), way_send=(4,), way_recv=(4,), act_send=(8,), act_recv=(8,), res_send=(2,), res_recv=(2,),
         rs_send=(len(SUMS), 7), rs_recv=(len(SUMS), 5), vec_sem=(2,), idle_sem=(1,),
     )
     names = [*inputs, *small, *outputs, *scratch, *sems]

time: 262 us -> 257 us (0.981)
  Pallas kernels: 261 us -> 255 us
    pallas_call x1, Pallas kernels: 257 us -> 251 us  [relay_call(): pl.pallas_call(functools.partial(relay, names), out_shape=[jax.ShapeDtype...]
where the time goes in v2:
time: 257 us; the launch traced here: 256 us
  Pallas kernels  255 us (99%)
    pallas_call x1, Pallas kernels, relay_call(): pl.pallas_call(functools.partial(relay, names), out_shape=[jax.ShapeDtype...  251 us

profile of v2, /device:TPU:0, one launch (start us, length us, event | category | flops | bytes accessed | tf_op | source)
XLA Modules:
  0.0 256.1 jit_solution(9840416667858530057)
XLA Ops:
  0.7 251.2 %relay.1 = (bf16[128,1024]{1,0:T(8,128)(2,1)}, bf16[128,1024]{1,0:T(8,128)(2,1)}, f32[64,3072]{1,0:T(8,128)}, f32[64,1024]{1,0:T(8,128)}, f32[64,4096]{1,0:T(8,1...) custom-call(bf16[128,1024]{1,0:T(8,128)(2,1)} %bitcast.10, bf16[128,1024]{1,0:T(8,128)(2,1)} %bitcast.11, ...), custom_call_target="tpu_custom_call" | custom-call | tf_op jit(solution)/shard_map/relay/pallas_call | solution.py:1104
  251.9 4.1 %hand_over.1 = (bf16[1,2,64,1024]{3,2,1,0:T(8,128)(2,1)}, bf16[1,2,64,1024]{3,2,1,0:T(8,128)(2,1)}, f32[1,64,3072]{2,1,0:T(8,128)}, f32[1,64,1024]{2,1,0:T(8,128...) custom-call(bf16[128,1024]{1,0:T(8,128)(2,1)} %get-tuple-element.33., ...), custom_call_target="tpu_custom_call" | custom-call | tf_op jit(solution)/shard_map/hand_over/pallas_call | solution.py:1147

commit v3 on v2

--- a/solution.py
+++ b/solution.py
@@ -968,15 +968,15 @@
                 issue_near(0)
                 issue(1)
                 issue_near(1)
+                issue(2)
+                issue(3)
 
             main(backward_dh)
             exchange_when(leading, DB)
 
             @grads
             def _():
-                issue(2)
                 issue_near(2)
-                issue(3)
                 exchanged(flow, C, DU)
                 grad_of(2, C, DU)
 

time: 257 us -> 257 us (level)
  no operation moved by 1% of the time
where the time goes in v3:
time: 257 us; the launch traced here: 256 us
  Pallas kernels  255 us (99%)
    pallas_call x1, Pallas kernels, relay_call(): pl.pallas_call(functools.partial(relay, names), out_shape=[jax.ShapeDtype...  251 us

profile of v3, /device:TPU:0, one launch (start us, length us, event | category | flops | bytes accessed | tf_op | source)
XLA Modules:
  0.0 256.1 jit_solution(16368693682070802951)
XLA Ops:
  0.7 251.2 %relay.1 = (bf16[128,1024]{1,0:T(8,128)(2,1)}, bf16[128,1024]{1,0:T(8,128)(2,1)}, f32[64,3072]{1,0:T(8,128)}, f32[64,1024]{1,0:T(8,128)}, f32[64,4096]{1,0:T(8,1...) custom-call(bf16[128,1024]{1,0:T(8,128)(2,1)} %bitcast.10, bf16[128,1024]{1,0:T(8,128)(2,1)} %bitcast.11, ...), custom_call_target="tpu_custom_call" | custom-call | tf_op jit(solution)/shard_map/relay/pallas_call | solution.py:1104
  251.8 4.1 %hand_over.1 = (bf16[1,2,64,1024]{3,2,1,0:T(8,128)(2,1)}, bf16[1,2,64,1024]{3,2,1,0:T(8,128)(2,1)}, f32[1,64,3072]{2,1,0:T(8,128)}, f32[1,64,1024]{2,1,0:T(8,128...) custom-call(bf16[128,1024]{1,0:T(8,128)(2,1)} %get-tuple-element.33., ...), custom_call_target="tpu_custom_call" | custom-call | tf_op jit(solution)/shard_map/hand_over/pallas_call | solution.py:1147
